TPU v7x, 512 devices: a whole 4x8x8 slice. The times are simulated.
512 devices in a mesh: dom: 32 (over z, x), tm: 16 (over y, core).
Axes of the slice: x: 4, y: 8, z: 8, core: 2. Of those that a mesh axis runs over, the one named last changes fastest.
Arguments:
- signal: bfloat16 [8, 512, 65536], P(None, 'tm', 'dom'), may hold values from -6 to 6
- weights: bfloat16 [512, 5, 128, 128], P('dom'), may hold values from 0 to 10.5, as said below
- send_list: int32 [32, 4, 3], P('dom'), may hold values from 0 to 15, as said below
- col_ref: int32 [512, 5], P('dom'), may hold values from 0 to 27, as said below
- kernel: bfloat16 [512, 512], P('tm'), may hold values from -0.2 to 1.6
- cheb_coef: float32 [3], replicated, may hold values from 0.5 to 1.5
Outputs:
- filtered: bfloat16 [8, 512, 65536], P(None, 'tm', 'dom')
Inputs may be any that keep to these rules, and one draw needn't show every extreme that they name: `send_list`: for each q and k the 3 entries are distinct block rows of partition q. col_ref[g, 0] = g % 16. An entry e >= 16 of partition p names partition q = p + d_k (k = (e - 16) // 3), which always exists; for each p and k the slots s used run from 0 up to some count of at most 3, every such slot is used by some block row of p, and some partition uses all 3 from some k. `weights`: Nonnegative; every diagonal entry of slot 0 blocks is 0.5 or more.
All inputs are finite; a program needn't handle non-finite values.
Results may differ from a plain program's by a relative error of at most 0.023.
Values may be sent and summed in bfloat16 or wider, within the bound.
No kernel may reach another device: no remote copies, remote signals or barrier semaphores. Data moves between devices by JAX's collectives and lax.ppermute only.
A program may use at most 64 MiB of HBM per device.

v0:
```python
import jax
import jax.numpy as jnp
from jax import lax
from jax.sharding import PartitionSpec as P

REACH = 2


def from_behind(block, axis, distance):
    devices = range(lax.axis_size(axis))
    route = [(i - distance, i) for i in devices if i - distance in devices]
    return lax.ppermute(block, axis, route)


def body(signal, weights, send_list, col_ref, kernel, cheb_coef):
    probes, t_loc, n_loc = signal.shape
    blocks_here = weights.shape[0]
    block_size = weights.shape[2]
    row_count = probes * t_loc
    degree = jnp.sum(weights, axis=(1, 3), dtype=jnp.float32)
    inv_root = lax.rsqrt(degree)[:, None, :]
    signal_blocks = signal.reshape(row_count, blocks_here, block_size).transpose(1, 0, 2)
    offsets = list(range(-REACH, 0)) + list(range(1, REACH + 1))
    send_rows = send_list[0]

    def neighbour_product(field):
        scaled = (field.astype(jnp.float32) * inv_root).astype(jnp.bfloat16)
        received = []
        for way_index, distance in enumerate(offsets):
            outgoing = jnp.take(scaled, send_rows[way_index], axis=0)
            received.append(from_behind(outgoing, "dom", -distance))
        source = jnp.concatenate([scaled] + received, axis=0)
        picked = jnp.take(source, col_ref, axis=0)
        return jnp.einsum("bjrm,bjnm->brn", picked, weights, preferred_element_type=jnp.float32)

    first_sum = neighbour_product(signal_blocks)
    term_one = (-inv_root * first_sum).astype(jnp.bfloat16)
    second_sum = neighbour_product(term_one)
    term_two = (-2.0 * inv_root * second_sum - signal_blocks.astype(jnp.float32)).astype(
        jnp.bfloat16
    )
    combined_field = (
        cheb_coef[0] * signal_blocks.astype(jnp.float32)
        + cheb_coef[1] * term_one.astype(jnp.float32)
        + cheb_coef[2] * term_two.astype(jnp.float32)
    ).astype(jnp.bfloat16)
    time_whole = lax.all_to_all(
        combined_field.transpose(1, 0, 2).reshape(probes, t_loc, n_loc),
        "tm",
        split_axis=2,
        concat_axis=1,
        tiled=True,
    )
    filtered_whole = jnp.einsum(
        "ut,ptn->pun",
        lax.all_gather(kernel, "tm", axis=0, tiled=True),
        time_whole,
        preferred_element_type=jnp.float32,
    ).astype(jnp.bfloat16)
    return lax.all_to_all(filtered_whole, "tm", split_axis=1, concat_axis=2, tiled=True)


def solution(mesh):
    in_specs = (
        P(None, "tm", "dom"),
        P("dom", None, None, None),
        P("dom", None, None),
        P("dom", None),
        P("tm", None),
        P(),
    )
    out_specs = P(None, "tm", "dom")
    return jax.shard_map(body, mesh=mesh, in_specs=in_specs, out_specs=out_specs, check_vma=False)
```

profile of v0, /device:TPU:135, one launch (start us, length us, event | category | flops | bytes accessed | tf_op | source)
XLA Modules:
  0.0 193.9 jit_solution(8609952959684335362)
XLA Ops:
  0.0 1.2 slice_reduce_fusion
  1.2 2.2 %convert_reduce_fusion = f32[16,128]{1,0:T(8,128)S(1)} fusion(bf16[16,5,128,128]{3,2,1,0:T(8,128)(2,1)} %param.11), kind=kLoop, calls=%fused_computation.14 | loop fusion | flops 2619392 | bytes 2629632 | tf_op jit(solution)/shard_map/reduce_sum | solution.py:20
  3.4 0.0 copy-done.1
  3.4 0.3 copy.58
  3.7 0.0 copy-start
  3.7 0.8 constant_dynamic-update-slice_fusion.4
  4.6 0.5 copy-done
  5.1 0.6 gather_fusion
  5.7 0.1 broadcast_select_fusion.7
  5.7 4.8 %collective-permute-start = (bf16[3,256,128]{2,1,0:T(8,128)(2,1)S(1)}, bf16[3,256,128]{2,1,0:T(8,128)(2,1)S(1)}, u32[]{:S(2)}, u32[]{:S(2)}) collective-permute-start(bf16[3,256,128]{2,1,0:T(8,128)(2,1)S(1)} %broadcast_select_fusion.7), channel_id=1, source_target_pairs={{0,32},{16,48},{32,64},{48,80},{64,96},{80,112},{96,128},{112,144}... | collective-permute-start | bytes 589832 | tf_op jit(solution)/shard_map/ppermute | solution.py:12
  10.6 0.6 gather_fusion.1
  11.2 0.8 broadcast_select_fusion.5
  12.0 3.7 %collective-permute-start.1 = (bf16[3,256,128]{2,1,0:T(8,128)(2,1)}, bf16[3,256,128]{2,1,0:T(8,128)(2,1)}, u32[]{:S(2)}, u32[]{:S(2)}) collective-permute-start(bf16[3,256,128]{2,1,0:T(8,128)(2,1)} %broadcast_select_fusion.5), channel_id=1, source_target_pairs={{0,16},{16,32},{32,48},{48,64},{64,80},{80,96},{96,112},{112,128},... | collective-permute-start | bytes 589832 | tf_op jit(solution)/shard_map/ppermute | solution.py:12
  15.7 0.6 gather_fusion.2
  16.3 0.8 broadcast_select_fusion.3
  17.1 1.9 collective-permute-start.2
  19.0 0.6 gather_fusion.3
  19.6 0.1 broadcast_select_fusion.1
  19.7 1.9 collective-permute-start.3
  21.6 0.0 copy-done.3
  21.7 0.1 copy.38
  21.8 0.1 reshape.139
  21.8 0.1 copy.36
  21.9 0.7 fusion.26
  22.6 0.0 collective-permute-done
  22.7 0.0 collective-permute-done.1
  22.7 1.0 constant_dynamic-update-slice_fusion.2
  23.6 2.9 %collective-permute-done.2 = bf16[3,256,128]{2,1,0:T(8,128)(2,1)} collective-permute-done((bf16[3,256,128]{2,1,0:T(8,128)(2,1)}, bf16[3,256,128]{2,1,0:T(8,128)(2,1)}, u32[]{:S(2)}, u32[]{:S(2)}) %collective-permute-start.2) | collective-permute-done | bytes 196640 | tf_op jit(solution)/shard_map/ppermute | solution.py:12
  26.6 1.0 constant_dynamic-update-slice_fusion.1
  27.5 2.8 %collective-permute-done.3 = bf16[3,256,128]{2,1,0:T(8,128)(2,1)S(1)} collective-permute-done((bf16[3,256,128]{2,1,0:T(8,128)(2,1)S(1)}, bf16[3,256,128]{2,1,0:T(8,128)(2,1)S(1)}, u32[]{:S(2)}, u32[]{:S(2)}) %collective-permute-start.3) | collective-permute-done | bytes 196640 | tf_op jit(solution)/shard_map/ppermute | solution.py:12
  30.3 5.7 %gather_fusion.4 = bf16[80,256,128]{2,1,0:T(8,128)(2,1)} fusion(bf16[28,256,128]{2,1,0:T(8,128)(2,1)S(1)} %constant_dynamic-update-slice_fusion, s32[1024]{0:T(1024)S(1)} %pad_clamp_fusion), kind=kCustom, calls=%fused_computation.1.clone | custom fusion | bytes 10486080 | tf_op jit(solution)/shard_map/jit(_take)/gather | solution.py:33
  36.0 6.2 %constant_dynamic-update-slice_fusion.9 = (bf16[28,256,128]{2,1,0:T(8,128)(2,1)S(1)}, bf16[16,256,128]{2,1,0:T(8,128)(2,1)}, bf16[16,256,128]{2,1,0:T(8,128)(2,1)}) fusion(f32[16,128]{1,0:T(8,128)S(1)} %get-tuple-element.17, bf16[16,5,128,128]{3,2,1,0:T(8,128)(2,1)} %param.11, bf16[16,5,256,128]{3,2,1,0:T(8,128)(2,1)} %bitcast.65, ...), kind=kOutput, calls=%fused_computation.53 | convolution fusion | flops 676331520 | bytes 11026512 | tf_op jit(solution)/shard_map/bjrm,bjnm->brn/dot_general | solution.py:34
  42.2 1.8 gather_fusion.5
  44.0 1.8 gather_fusion.6
  45.8 1.8 gather_fusion.7
  47.7 1.8 gather_fusion.8
  49.5 0.1 broadcast_select_fusion.6
  49.6 5.0 %collective-permute-start.4 = (bf16[3,256,128]{2,1,0:T(8,128)(2,1)S(1)}, bf16[3,256,128]{2,1,0:T(8,128)(2,1)S(1)}, u32[]{:S(2)}, u32[]{:S(2)}) collective-permute-start(bf16[3,256,128]{2,1,0:T(8,128)(2,1)S(1)} %broadcast_select_fusion.6), channel_id=1, source_target_pairs={{0,32},{16,48},{32,64},{48,80},{64,96},{80,112},{96,128},{112,144}... | collective-permute-start | bytes 589832 | tf_op jit(solution)/shard_map/ppermute | solution.py:12
  54.6 0.1 broadcast_select_fusion.4
  54.7 6.4 %collective-permute-start.5 = (bf16[3,256,128]{2,1,0:T(8,128)(2,1)S(1)}, bf16[3,256,128]{2,1,0:T(8,128)(2,1)S(1)}, u32[]{:S(2)}, u32[]{:S(2)}) collective-permute-start(bf16[3,256,128]{2,1,0:T(8,128)(2,1)S(1)} %broadcast_select_fusion.4), channel_id=1, source_target_pairs={{0,16},{16,32},{32,48},{48,64},{64,80},{80,96},{96,112},{112,128},... | collective-permute-start | bytes 589832 | tf_op jit(solution)/shard_map/ppermute | solution.py:12
  61.0 0.1 broadcast_select_fusion.2
  61.1 1.9 collective-permute-start.6
  63.1 0.1 broadcast_select_fusion
  63.2 2.1 %collective-permute-start.7 = (bf16[3,256,128]{2,1,0:T(8,128)(2,1)S(1)}, bf16[3,256,128]{2,1,0:T(8,128)(2,1)S(1)}, u32[]{:S(2)}, u32[]{:S(2)}) collective-permute-start(bf16[3,256,128]{2,1,0:T(8,128)(2,1)S(1)} %broadcast_select_fusion), channel_id=1, source_target_pairs={{32,0},{48,16},{64,32},{80,48},{96,64},{112,80},{128,96},{144,112}... | collective-permute-start | bytes 589832 | tf_op jit(solution)/shard_map/ppermute | solution.py:12
  65.3 0.0 collective-permute-done.4
  65.3 0.0 collective-permute-done.5
  65.4 4.3 %collective-permute-done.6 = bf16[3,256,128]{2,1,0:T(8,128)(2,1)S(1)} collective-permute-done((bf16[3,256,128]{2,1,0:T(8,128)(2,1)S(1)}, bf16[3,256,128]{2,1,0:T(8,128)(2,1)S(1)}, u32[]{:S(2)}, u32[]{:S(2)}) %collective-permute-start.6) | collective-permute-done | bytes 196640 | tf_op jit(solution)/shard_map/ppermute | solution.py:12
  69.7 2.9 %collective-permute-done.7 = bf16[3,256,128]{2,1,0:T(8,128)(2,1)S(1)} collective-permute-done((bf16[3,256,128]{2,1,0:T(8,128)(2,1)S(1)}, bf16[3,256,128]{2,1,0:T(8,128)(2,1)S(1)}, u32[]{:S(2)}, u32[]{:S(2)}) %collective-permute-start.7) | collective-permute-done | bytes 196640 | tf_op jit(solution)/shard_map/ppermute | solution.py:12
  72.6 5.7 %gather_fusion.9 = bf16[80,256,128]{2,1,0:T(8,128)(2,1)} fusion(bf16[28,256,128]{2,1,0:T(8,128)(2,1)S(1)} %constant_dynamic-update-slice_fusion.5, s32[1024]{0:T(1024)S(1)} %pad_clamp_fusion), kind=kCustom, calls=%fused_computation.9.clone | custom fusion | bytes 10486080 | tf_op jit(solution)/shard_map/jit(_take)/gather | solution.py:33
  78.2 8.2 %fusion.11 = bf16[256,16,128]{2,0,1:T(8,128)(2,1)S(1)} fusion(bf16[16,256,128]{2,1,0:T(8,128)(2,1)} %get-tuple-element.21, f32[256,16,128]{2,1,0:T(8,128)} %bitcast.63, bf16[16,5,128,128]{3,2,1,0:T(8,128)(2,1)} %param.11, bf16[16,5,256,128]{3,2,1,0:T(8,128)(2,1)} %bitcast.64, pred[16,5]{1,0:T(8,128)(4,1)S(1)} %copy.36, ...), kind=kOutput, calls=%fused_computation.24 | convolution fusion | flops 679477248 | bytes 12066908 | tf_op jit(solution)/shard_map/bjrm,bjnm->brn/dot_general | solution.py:34
  86.5 0.5 copy.53
  87.0 3.4 %reshape.158 = bf16[8,32,2048]{1,0,2:T(8,128)(2,1)} reshape(bf16[256,16,128]{0,2,1:T(8,128)(2,1)S(1)} %copy.53) | data formatting | bytes 2097152 | tf_op jit(solution)/shard_map/reshape | solution.py:48
  90.4 7.4 %reshape.163 = bf16[16,2,16384]{2,1,0:T(2,128)(2,1)} reshape(bf16[2048,8,32]{2,1,0:T(8,128)(2,1)} %bitcast.60) | data formatting | bytes 2097152
  97.8 11.5 %all-to-all-start = ((bf16[16,2,16384]{2,1,0:T(2,128)(2,1)}), bf16[16,2,16384]{2,1,0:T(2,128)(2,1)S(1)}, u32[]{:S(2)}, u32[]{:S(2)}) async-start(bf16[16,2,16384]{2,1,0:T(2,128)(2,1)} %reshape.163), calls=%async_computation | async-start | bytes 2097152 | tf_op jit(solution)/shard_map/all_to_all | solution.py:47
  109.4 0.0 copy-done.2
  109.4 38.6 %all_gather.3 = bf16[512,512]{1,0:T(8,128)(2,1)S(1)} all-gather(bf16[32,512]{1,0:T(8,128)(2,1)S(1)} %copy-done.2), channel_id=1, replica_groups=mesh['dom'=32,'tm'=16] {'tm'}, dimensions={0}, use_global_device_ids=true | all-gather | bytes 557056 | tf_op jit(solution)/shard_map/all_gather | solution.py:56
  148.0 0.0 all-to-all-done
  148.0 3.5 %reshape.164 = bf16[2048,8,32]{2,1,0:T(8,128)(2,1)} reshape(bf16[16,2,16384]{2,1,0:T(2,128)(2,1)S(1)} %all-to-all-done) | data formatting | bytes 2097152
  151.5 4.5 %copy.45 = bf16[8,16,32,128]{3,2,1,0:T(8,128)(2,1)S(1)} copy(bf16[8,16,32,128]{2,0,3,1:T(8,128)(2,1)} %bitcast.61) | data formatting | bytes 2097152 | tf_op jit(solution)/shard_map/all_to_all | solution.py:47
  156.1 0.8 fusion.19
  156.8 0.8 copy.47
  157.6 34.3 %all_to_all.36 = bf16[8,512,128]{2,0,1:T(8,128)(2,1)S(1)} all-to-all(bf16[8,512,128]{2,0,1:T(8,128)(2,1)S(1)} %copy.47), channel_id=1, replica_groups=mesh['dom'=32,'tm'=16] {'tm'}, dimensions={1} | all-to-all | bytes 2097152 | tf_op jit(solution)/shard_map/all_to_all | solution.py:60
  191.9 0.7 copy.49
  192.6 1.3 all_to_all.33
  (25 shorter events, 0.3 us)
Async XLA Ops:
  0.0 3.4 %copy-start.1 = (bf16[8,32,2048]{2,1,0:T(8,128)(2,1)S(1)}, bf16[8,32,2048]{2,1,0:T(8,128)(2,1)}, u32[]{:S(2)}) copy-start(bf16[8,32,2048]{2,1,0:T(8,128)(2,1)} %param.10) | copy-start | bytes 3145732
  3.7 1.4 copy-start
  5.1 16.6 %copy-start.3 = (s32[16,5]{0,1:T(8,128)S(1)}, s32[16,5]{0,1:T(8,128)}, u32[]{:S(2)}) copy-start(s32[16,5]{0,1:T(8,128)} %param.13) | copy-start | bytes 964
  5.1 16.9 %copy-start.4 = (f32[3]{0:T(128)S(1)}, f32[3]{0:T(128)}, u32[]{:S(2)}) copy-start(f32[3]{0:T(128)} %param.15) | copy-start | bytes 40
  5.7 16.9 %collective-permute-start = (bf16[3,256,128]{2,1,0:T(8,128)(2,1)S(1)}, bf16[3,256,128]{2,1,0:T(8,128)(2,1)S(1)}, u32[]{:S(2)}, u32[]{:S(2)}) collective-permute-start(bf16[3,256,128]{2,1,0:T(8,128)(2,1)S(1)} %broadcast_select_fusion.7), channel_id=1, source_target_pairs={{0,32},{16,48},{32,64},{48,80},{64,96},{80,112},{96,128},{112,144}... | collective-permute-start | bytes 589832 | tf_op jit(solution)/shard_map/ppermute | solution.py:12
  12.0 10.7 %collective-permute-start.1 = (bf16[3,256,128]{2,1,0:T(8,128)(2,1)}, bf16[3,256,128]{2,1,0:T(8,128)(2,1)}, u32[]{:S(2)}, u32[]{:S(2)}) collective-permute-start(bf16[3,256,128]{2,1,0:T(8,128)(2,1)} %broadcast_select_fusion.5), channel_id=1, source_target_pairs={{0,16},{16,32},{32,48},{48,64},{64,80},{80,96},{96,112},{112,128},... | collective-permute-start | bytes 589832 | tf_op jit(solution)/shard_map/ppermute | solution.py:12
  17.1 9.5 %collective-permute-start.2 = (bf16[3,256,128]{2,1,0:T(8,128)(2,1)}, bf16[3,256,128]{2,1,0:T(8,128)(2,1)}, u32[]{:S(2)}, u32[]{:S(2)}) collective-permute-start(bf16[3,256,128]{2,1,0:T(8,128)(2,1)} %broadcast_select_fusion.3), channel_id=1, source_target_pairs={{16,0},{32,16},{48,32},{64,48},{80,64},{96,80},{112,96},{128,112},... | collective-permute-start | bytes 589832 | tf_op jit(solution)/shard_map/ppermute | solution.py:12
  19.7 10.6 %collective-permute-start.3 = (bf16[3,256,128]{2,1,0:T(8,128)(2,1)S(1)}, bf16[3,256,128]{2,1,0:T(8,128)(2,1)S(1)}, u32[]{:S(2)}, u32[]{:S(2)}) collective-permute-start(bf16[3,256,128]{2,1,0:T(8,128)(2,1)S(1)} %broadcast_select_fusion.1), channel_id=1, source_target_pairs={{32,0},{48,16},{64,32},{80,48},{96,64},{112,80},{128,96},{144,112}... | collective-permute-start | bytes 589832 | tf_op jit(solution)/shard_map/ppermute | solution.py:12
  49.6 15.7 %collective-permute-start.4 = (bf16[3,256,128]{2,1,0:T(8,128)(2,1)S(1)}, bf16[3,256,128]{2,1,0:T(8,128)(2,1)S(1)}, u32[]{:S(2)}, u32[]{:S(2)}) collective-permute-start(bf16[3,256,128]{2,1,0:T(8,128)(2,1)S(1)} %broadcast_select_fusion.6), channel_id=1, source_target_pairs={{0,32},{16,48},{32,64},{48,80},{64,96},{80,112},{96,128},{112,144}... | collective-permute-start | bytes 589832 | tf_op jit(solution)/shard_map/ppermute | solution.py:12
  54.7 10.7 %collective-permute-start.5 = (bf16[3,256,128]{2,1,0:T(8,128)(2,1)S(1)}, bf16[3,256,128]{2,1,0:T(8,128)(2,1)S(1)}, u32[]{:S(2)}, u32[]{:S(2)}) collective-permute-start(bf16[3,256,128]{2,1,0:T(8,128)(2,1)S(1)} %broadcast_select_fusion.4), channel_id=1, source_target_pairs={{0,16},{16,32},{32,48},{48,64},{64,80},{80,96},{96,112},{112,128},... | collective-permute-start | bytes 589832 | tf_op jit(solution)/shard_map/ppermute | solution.py:12
  61.1 8.5 %collective-permute-start.6 = (bf16[3,256,128]{2,1,0:T(8,128)(2,1)S(1)}, bf16[3,256,128]{2,1,0:T(8,128)(2,1)S(1)}, u32[]{:S(2)}, u32[]{:S(2)}) collective-permute-start(bf16[3,256,128]{2,1,0:T(8,128)(2,1)S(1)} %broadcast_select_fusion.2), channel_id=1, source_target_pairs={{16,0},{32,16},{48,32},{64,48},{80,64},{96,80},{112,96},{128,112},... | collective-permute-start | bytes 589832 | tf_op jit(solution)/shard_map/ppermute | solution.py:12
  63.2 9.4 %collective-permute-start.7 = (bf16[3,256,128]{2,1,0:T(8,128)(2,1)S(1)}, bf16[3,256,128]{2,1,0:T(8,128)(2,1)S(1)}, u32[]{:S(2)}, u32[]{:S(2)}) collective-permute-start(bf16[3,256,128]{2,1,0:T(8,128)(2,1)S(1)} %broadcast_select_fusion), channel_id=1, source_target_pairs={{32,0},{48,16},{64,32},{80,48},{96,64},{112,80},{128,96},{144,112}... | collective-permute-start | bytes 589832 | tf_op jit(solution)/shard_map/ppermute | solution.py:12
  97.8 11.5 %copy-start.2 = (bf16[32,512]{1,0:T(8,128)(2,1)S(1)}, bf16[32,512]{1,0:T(8,128)(2,1)}, u32[]{:S(2)}) copy-start(bf16[32,512]{1,0:T(8,128)(2,1)} %param.14) | copy-start | bytes 98308
  97.8 50.2 %all-to-all-start = ((bf16[16,2,16384]{2,1,0:T(2,128)(2,1)}), bf16[16,2,16384]{2,1,0:T(2,128)(2,1)S(1)}, u32[]{:S(2)}, u32[]{:S(2)}) async-start(bf16[16,2,16384]{2,1,0:T(2,128)(2,1)} %reshape.163), calls=%async_computation | async-start | bytes 2097152 | tf_op jit(solution)/shard_map/all_to_all | solution.py:47
where the time goes:
time: 195 us; the launch traced here: 194 us
  blocking collectives  73 us (37%)
  local copies, waits for them, and re-layouts  47.9 us (25%)
  starting transfers between devices  39.3 us (20%)
  matrix products  15.2 us (8%)
  waiting for transfers between devices  12.9 us (7%)
  other arithmetic  5.12 us (3%)
    all_gather x1, blocking collectives, body(): lax.all_gather(kernel, 'tm', axis=0, tiled=True)  38.6 us
    all_to_all x1, blocking collectives, body(): lax.all_to_all(filtered_whole, 'tm', split_axis=1, concat_axis=2, tiled=T...  34.3 us
    ppermute x8, starting transfers between devices, from_behind(): return lax.ppermute(block, axis, route)  27.8 us
    dot_general x2, matrix products, neighbour_product(): jnp.einsum('bjrm,bjnm->brn', picked, weights, preferred_element_type=jnp....  14.4 us
    unnamed x19, local copies, waits for them, and re-layouts  13.8 us
    ppermute x8, waiting for transfers between devices, from_behind(): return lax.ppermute(block, axis, route)  12.9 us
    all_to_all x1, starting transfers between devices, body(): lax.all_to_all(combined_field.transpose(1, 0, 2).reshape(probes, t_loc, n...  11.5 us
    gather x2, local copies, waits for them, and re-layouts, neighbour_product(): picked = jnp.take(source, col_ref, axis=0)  11.3 us
  transfers between devices with their start and end apart: 9, of which 4 were waited for; matrix products, arithmetic and copies ran while one was open for 3% of the time, Pallas kernels for 0%

commit v1 on v0

--- a/solution.py
+++ b/solution.py
@@ -44,12 +44,15 @@
         + cheb_coef[1] * term_one.astype(jnp.float32)
         + cheb_coef[2] * term_two.astype(jnp.float32)
     ).astype(jnp.bfloat16)
-    time_whole = lax.all_to_all(
-        combined_field.transpose(1, 0, 2).reshape(probes, t_loc, n_loc),
-        "tm",
-        split_axis=2,
-        concat_axis=1,
-        tiled=True,
+    s0 = combined_field.transpose(1, 0, 2).reshape(probes, t_loc, n_loc)
+    time_whole = jnp.concatenate(
+        lax.all_to_all(
+            jnp.stack(jnp.split(s0, lax.axis_size("tm"), 2), axis=0),
+            "tm",
+            concat_axis=0,
+            split_axis=0,
+        ),
+        1,
     )
     filtered_whole = jnp.einsum(
         "ut,ptn->pun",

time: 195 us -> 187 us (0.959)
  local copies, waits for them, and re-layouts: 47.9 us -> 40.2 us
    all_to_all x1 -> x0, local copies, waits for them, and re-layouts: 4.52 us -> none  [body(): lax.all_to_all(combined_field.transpose(1, 0, 2).reshape(probes, t_loc, n...]
    reshape x2, local copies, waits for them, and re-layouts: 3.89 us -> 0.59 us  [the longest x1 0.49 us: body(): s0 = combined_field.transpose(1, 0, 2).reshape(probes, t_loc, n_loc)]
    unnamed x19 -> x32, local copies, waits for them, and re-layouts: 13.8 us -> 12.5 us
  transfers between devices with their start and end apart: 9 -> 9, of which waited for: 4 -> 4; matrix products, arithmetic and copies ran while one was open for 3% -> 4% of each run, Pallas kernels for 0% -> 0%
where the time goes in v1:
time: 187 us; the launch traced here: 186 us
  blocking collectives  73 us (39%)
  local copies, waits for them, and re-layouts  40.2 us (21%)
  starting transfers between devices  39 us (21%)
  matrix products  15.2 us (8%)
  waiting for transfers between devices  13.1 us (7%)
  other arithmetic  5.12 us (3%)
    all_gather x1, blocking collectives, body(): lax.all_gather(kernel, 'tm', axis=0, tiled=True)  38.6 us
    all_to_all x1, blocking collectives, body(): lax.all_to_all(filtered_whole, 'tm', split_axis=1, concat_axis=2, tiled=T...  34.3 us
    ppermute x8, starting transfers between devices, from_behind(): return lax.ppermute(block, axis, route)  27.6 us
    dot_general x2, matrix products, neighbour_product(): jnp.einsum('bjrm,bjnm->brn', picked, weights, preferred_element_type=jnp....  14.4 us
    ppermute x8, waiting for transfers between devices, from_behind(): return lax.ppermute(block, axis, route)  13.1 us
    unnamed x32, local copies, waits for them, and re-layouts  12.5 us
    all_to_all x1, starting transfers between devices, body(): lax.all_to_all(jnp.stack(jnp.split(s0, lax.axis_size('tm'), 2), axis=0),...  11.4 us
    gather x2, local copies, waits for them, and re-layouts, neighbour_product(): picked = jnp.take(source, col_ref, axis=0)  11.3 us
  transfers between devices with their start and end apart: 9, of which 4 were waited for; matrix products, arithmetic and copies ran while one was open for 4% of the time, Pallas kernels for 0%

profile of v1, /device:TPU:135, one launch (start us, length us, event | category | flops | bytes accessed | tf_op | source)
XLA Modules:
  0.0 186.0 jit_solution(3094164349619691451)
XLA Ops:
  0.0 1.2 slice_reduce_fusion
  1.2 2.2 %convert_reduce_fusion = f32[16,128]{1,0:T(8,128)S(1)} fusion(bf16[16,5,128,128]{3,2,1,0:T(8,128)(2,1)} %param.11), kind=kLoop, calls=%fused_computation.14 | loop fusion | flops 2619392 | bytes 2629632 | tf_op jit(solution)/shard_map/reduce_sum | solution.py:20
  3.4 0.3 copy.67
  3.7 0.8 constant_dynamic-update-slice_fusion.4
  4.6 0.5 copy-done
  5.1 0.6 gather_fusion
  5.7 4.8 %collective-permute-start = (bf16[3,256,128]{2,1,0:T(8,128)(2,1)S(1)}, bf16[3,256,128]{2,1,0:T(8,128)(2,1)S(1)}, u32[]{:S(2)}, u32[]{:S(2)}) collective-permute-start(bf16[3,256,128]{2,1,0:T(8,128)(2,1)S(1)} %broadcast_select_fusion.7), channel_id=1, source_target_pairs={{0,32},{16,48},{32,64},{48,80},{64,96},{80,112},{96,128},{112,144}... | collective-permute-start | bytes 589832 | tf_op jit(solution)/shard_map/ppermute | solution.py:12
  10.6 0.6 gather_fusion.1
  11.2 0.8 broadcast_select_fusion.5
  12.0 3.7 %collective-permute-start.1 = (bf16[3,256,128]{2,1,0:T(8,128)(2,1)}, bf16[3,256,128]{2,1,0:T(8,128)(2,1)}, u32[]{:S(2)}, u32[]{:S(2)}) collective-permute-start(bf16[3,256,128]{2,1,0:T(8,128)(2,1)} %broadcast_select_fusion.5), channel_id=1, source_target_pairs={{0,16},{16,32},{32,48},{48,64},{64,80},{80,96},{96,112},{112,128},... | collective-permute-start | bytes 589832 | tf_op jit(solution)/shard_map/ppermute | solution.py:12
  15.7 0.6 gather_fusion.2
  16.3 0.8 broadcast_select_fusion.3
  17.1 1.9 %collective-permute-start.2 = (bf16[3,256,128]{2,1,0:T(8,128)(2,1)}, bf16[3,256,128]{2,1,0:T(8,128)(2,1)}, u32[]{:S(2)}, u32[]{:S(2)}) collective-permute-start(bf16[3,256,128]{2,1,0:T(8,128)(2,1)} %broadcast_select_fusion.3), channel_id=1, source_target_pairs={{16,0},{32,16},{48,32},{64,48},{80,64},{96,80},{112,96},{128,112},... | collective-permute-start | bytes 589832 | tf_op jit(solution)/shard_map/ppermute | solution.py:12
  19.0 0.6 gather_fusion.3
  19.7 1.9 %collective-permute-start.3 = (bf16[3,256,128]{2,1,0:T(8,128)(2,1)S(1)}, bf16[3,256,128]{2,1,0:T(8,128)(2,1)S(1)}, u32[]{:S(2)}, u32[]{:S(2)}) collective-permute-start(bf16[3,256,128]{2,1,0:T(8,128)(2,1)S(1)} %broadcast_select_fusion.1), channel_id=1, source_target_pairs={{32,0},{48,16},{64,32},{80,48},{96,64},{112,80},{128,96},{144,112}... | collective-permute-start | bytes 589832 | tf_op jit(solution)/shard_map/ppermute | solution.py:12
  21.8 0.1 copy.51
  21.9 0.7 fusion.42
  22.7 1.0 constant_dynamic-update-slice_fusion.2
  23.6 2.9 %collective-permute-done.2 = bf16[3,256,128]{2,1,0:T(8,128)(2,1)} collective-permute-done((bf16[3,256,128]{2,1,0:T(8,128)(2,1)}, bf16[3,256,128]{2,1,0:T(8,128)(2,1)}, u32[]{:S(2)}, u32[]{:S(2)}) %collective-permute-start.2) | collective-permute-done | bytes 196640 | tf_op jit(solution)/shard_map/ppermute | solution.py:12
  26.6 1.0 constant_dynamic-update-slice_fusion.1
  27.5 2.8 %collective-permute-done.3 = bf16[3,256,128]{2,1,0:T(8,128)(2,1)S(1)} collective-permute-done((bf16[3,256,128]{2,1,0:T(8,128)(2,1)S(1)}, bf16[3,256,128]{2,1,0:T(8,128)(2,1)S(1)}, u32[]{:S(2)}, u32[]{:S(2)}) %collective-permute-start.3) | collective-permute-done | bytes 196640 | tf_op jit(solution)/shard_map/ppermute | solution.py:12
  30.3 5.7 %gather_fusion.4 = bf16[80,256,128]{2,1,0:T(8,128)(2,1)} fusion(bf16[28,256,128]{2,1,0:T(8,128)(2,1)S(1)} %constant_dynamic-update-slice_fusion, s32[1024]{0:T(1024)S(1)} %pad_clamp_fusion), kind=kCustom, calls=%fused_computation.1.clone | custom fusion | bytes 10486080 | tf_op jit(solution)/shard_map/jit(_take)/gather | solution.py:33
  36.0 6.2 %constant_dynamic-update-slice_fusion.9 = (bf16[28,256,128]{2,1,0:T(8,128)(2,1)S(1)}, bf16[16,256,128]{2,1,0:T(8,128)(2,1)}, bf16[16,256,128]{2,1,0:T(8,128)(2,1)}) fusion(f32[16,128]{1,0:T(8,128)S(1)} %get-tuple-element.17, bf16[16,5,128,128]{3,2,1,0:T(8,128)(2,1)} %param.11, bf16[16,5,256,128]{3,2,1,0:T(8,128)(2,1)} %bitcast.120, ...), kind=kOutput, calls=%fused_computation.85 | convolution fusion | flops 676331520 | bytes 11026512 | tf_op jit(solution)/shard_map/bjrm,bjnm->brn/dot_general | solution.py:34
  42.2 1.8 gather_fusion.5
  44.0 1.8 gather_fusion.6
  45.8 1.8 gather_fusion.7
  47.7 1.8 gather_fusion.8
  49.5 0.1 broadcast_select_fusion.6
  49.6 5.0 %collective-permute-start.4 = (bf16[3,256,128]{2,1,0:T(8,128)(2,1)S(1)}, bf16[3,256,128]{2,1,0:T(8,128)(2,1)S(1)}, u32[]{:S(2)}, u32[]{:S(2)}) collective-permute-start(bf16[3,256,128]{2,1,0:T(8,128)(2,1)S(1)} %broadcast_select_fusion.6), channel_id=1, source_target_pairs={{0,32},{16,48},{32,64},{48,80},{64,96},{80,112},{96,128},{112,144}... | collective-permute-start | bytes 589832 | tf_op jit(solution)/shard_map/ppermute | solution.py:12
  54.6 0.1 broadcast_select_fusion.4
  54.7 6.4 %collective-permute-start.5 = (bf16[3,256,128]{2,1,0:T(8,128)(2,1)S(1)}, bf16[3,256,128]{2,1,0:T(8,128)(2,1)S(1)}, u32[]{:S(2)}, u32[]{:S(2)}) collective-permute-start(bf16[3,256,128]{2,1,0:T(8,128)(2,1)S(1)} %broadcast_select_fusion.4), channel_id=1, source_target_pairs={{0,16},{16,32},{32,48},{48,64},{64,80},{80,96},{96,112},{112,128},... | collective-permute-start | bytes 589832 | tf_op jit(solution)/shard_map/ppermute | solution.py:12
  61.0 0.1 broadcast_select_fusion.2
  61.1 1.9 %collective-permute-start.6 = (bf16[3,256,128]{2,1,0:T(8,128)(2,1)S(1)}, bf16[3,256,128]{2,1,0:T(8,128)(2,1)S(1)}, u32[]{:S(2)}, u32[]{:S(2)}) collective-permute-start(bf16[3,256,128]{2,1,0:T(8,128)(2,1)S(1)} %broadcast_select_fusion.2), channel_id=1, source_target_pairs={{16,0},{32,16},{48,32},{64,48},{80,64},{96,80},{112,96},{128,112},... | collective-permute-start | bytes 589832 | tf_op jit(solution)/shard_map/ppermute | solution.py:12
  63.2 1.9 %collective-permute-start.7 = (bf16[3,256,128]{2,1,0:T(8,128)(2,1)S(1)}, bf16[3,256,128]{2,1,0:T(8,128)(2,1)S(1)}, u32[]{:S(2)}, u32[]{:S(2)}) collective-permute-start(bf16[3,256,128]{2,1,0:T(8,128)(2,1)S(1)} %broadcast_select_fusion), channel_id=1, source_target_pairs={{32,0},{48,16},{64,32},{80,48},{96,64},{112,80},{128,96},{144,112}... | collective-permute-start | bytes 589832 | tf_op jit(solution)/shard_map/ppermute | solution.py:12
  65.2 4.5 %collective-permute-done.6 = bf16[3,256,128]{2,1,0:T(8,128)(2,1)S(1)} collective-permute-done((bf16[3,256,128]{2,1,0:T(8,128)(2,1)S(1)}, bf16[3,256,128]{2,1,0:T(8,128)(2,1)S(1)}, u32[]{:S(2)}, u32[]{:S(2)}) %collective-permute-start.6) | collective-permute-done | bytes 196640 | tf_op jit(solution)/shard_map/ppermute | solution.py:12
  69.7 2.9 %collective-permute-done.7 = bf16[3,256,128]{2,1,0:T(8,128)(2,1)S(1)} collective-permute-done((bf16[3,256,128]{2,1,0:T(8,128)(2,1)S(1)}, bf16[3,256,128]{2,1,0:T(8,128)(2,1)S(1)}, u32[]{:S(2)}, u32[]{:S(2)}) %collective-permute-start.7) | collective-permute-done | bytes 196640 | tf_op jit(solution)/shard_map/ppermute | solution.py:12
  72.6 5.7 %gather_fusion.9 = bf16[80,256,128]{2,1,0:T(8,128)(2,1)} fusion(bf16[28,256,128]{2,1,0:T(8,128)(2,1)S(1)} %constant_dynamic-update-slice_fusion.5, s32[1024]{0:T(1024)S(1)} %pad_clamp_fusion), kind=kCustom, calls=%fused_computation.9.clone | custom fusion | bytes 10486080 | tf_op jit(solution)/shard_map/jit(_take)/gather | solution.py:33
  78.2 8.2 %fusion.11 = bf16[256,16,128]{2,0,1:T(8,128)(2,1)S(1)} fusion(bf16[16,256,128]{2,1,0:T(8,128)(2,1)} %get-tuple-element.21, f32[256,16,128]{2,1,0:T(8,128)} %bitcast.118, bf16[16,5,128,128]{3,2,1,0:T(8,128)(2,1)} %param.11, bf16[16,5,256,128]{3,2,1,0:T(8,128)(2,1)} %bitcast.119, pred[16,5]{1,0:T(8,128)(4,1)S(1)} %copy.51, ...), kind=kOutput, calls=%fused_computation.24 | convolution fusion | flops 679477248 | bytes 12066908 | tf_op jit(solution)/shard_map/bjrm,bjnm->brn/dot_general | solution.py:34
  86.5 0.7 copy.57
  87.2 0.5 reshape.43
  87.7 0.6 fusion.37
  88.3 0.6 fusion.36
  89.0 0.6 fusion.35
  89.6 0.6 fusion.34
  90.3 0.6 fusion.33
  90.9 0.6 fusion.32
  91.6 0.6 fusion.31
  92.2 0.6 fusion.30
  92.9 0.6 fusion.29
  93.5 0.6 fusion.28
  94.2 0.6 fusion.27
  94.8 0.6 fusion.26
  95.5 0.6 fusion.25
  96.1 0.6 fusion.24
  96.8 0.6 fusion.23
  97.4 0.6 fusion.22
  98.0 11.4 %all-to-all-start = ((bf16[16,8,32,128]{3,2,1,0:T(8,128)(2,1)}), bf16[16,8,32,128]{3,2,1,0:T(8,128)(2,1)S(1)}, u32[]{:S(2)}, u32[]{:S(2)}) async-start(bf16[16,8,32,128]{3,2,1,0:T(8,128)(2,1)} %fusion.22), calls=%async_computation | async-start | bytes 2097152 | tf_op jit(solution)/shard_map/all_to_all | solution.py:49
  109.4 38.6 %all_gather.3 = bf16[512,512]{1,0:T(8,128)(2,1)S(1)} all-gather(bf16[32,512]{1,0:T(8,128)(2,1)S(1)} %copy-done.2), channel_id=1, replica_groups=mesh['dom'=32,'tm'=16] {'tm'}, dimensions={0}, use_global_device_ids=true | all-gather | bytes 557056 | tf_op jit(solution)/shard_map/all_gather | solution.py:59
  148.1 0.1 copy.58
  148.2 0.8 fusion.19
  149.0 0.8 copy.60
  149.7 34.3 %all_to_all.23 = bf16[8,512,128]{2,0,1:T(8,128)(2,1)S(1)} all-to-all(bf16[8,512,128]{2,0,1:T(8,128)(2,1)S(1)} %copy.60), channel_id=1, replica_groups=mesh['dom'=32,'tm'=16] {'tm'}, dimensions={1} | all-to-all | bytes 2097152 | tf_op jit(solution)/shard_map/all_to_all | solution.py:63
  184.0 0.7 copy.62
  184.7 1.3 all_to_all.20
  (39 shorter events, 0.7 us)
Async XLA Ops:
  0.0 3.4 %copy-start.1 = (bf16[8,32,2048]{2,1,0:T(8,128)(2,1)S(1)}, bf16[8,32,2048]{2,1,0:T(8,128)(2,1)}, u32[]{:S(2)}) copy-start(bf16[8,32,2048]{2,1,0:T(8,128)(2,1)} %param.10) | copy-start | bytes 3145732
  3.7 1.4 copy-start
  5.1 16.6 %copy-start.3 = (s32[16,5]{0,1:T(8,128)S(1)}, s32[16,5]{0,1:T(8,128)}, u32[]{:S(2)}) copy-start(s32[16,5]{0,1:T(8,128)} %param.13) | copy-start | bytes 964
  5.1 16.9 %copy-start.4 = (f32[3]{0:T(128)S(1)}, f32[3]{0:T(128)}, u32[]{:S(2)}) copy-start(f32[3]{0:T(128)} %param.15) | copy-start | bytes 40
  5.7 16.9 %collective-permute-start = (bf16[3,256,128]{2,1,0:T(8,128)(2,1)S(1)}, bf16[3,256,128]{2,1,0:T(8,128)(2,1)S(1)}, u32[]{:S(2)}, u32[]{:S(2)}) collective-permute-start(bf16[3,256,128]{2,1,0:T(8,128)(2,1)S(1)} %broadcast_select_fusion.7), channel_id=1, source_target_pairs={{0,32},{16,48},{32,64},{48,80},{64,96},{80,112},{96,128},{112,144}... | collective-permute-start | bytes 589832 | tf_op jit(solution)/shard_map/ppermute | solution.py:12
  12.0 10.7 %collective-permute-start.1 = (bf16[3,256,128]{2,1,0:T(8,128)(2,1)}, bf16[3,256,128]{2,1,0:T(8,128)(2,1)}, u32[]{:S(2)}, u32[]{:S(2)}) collective-permute-start(bf16[3,256,128]{2,1,0:T(8,128)(2,1)} %broadcast_select_fusion.5), channel_id=1, source_target_pairs={{0,16},{16,32},{32,48},{48,64},{64,80},{80,96},{96,112},{112,128},... | collective-permute-start | bytes 589832 | tf_op jit(solution)/shard_map/ppermute | solution.py:12
  17.1 9.5 %collective-permute-start.2 = (bf16[3,256,128]{2,1,0:T(8,128)(2,1)}, bf16[3,256,128]{2,1,0:T(8,128)(2,1)}, u32[]{:S(2)}, u32[]{:S(2)}) collective-permute-start(bf16[3,256,128]{2,1,0:T(8,128)(2,1)} %broadcast_select_fusion.3), channel_id=1, source_target_pairs={{16,0},{32,16},{48,32},{64,48},{80,64},{96,80},{112,96},{128,112},... | collective-permute-start | bytes 589832 | tf_op jit(solution)/shard_map/ppermute | solution.py:12
  19.7 10.6 %collective-permute-start.3 = (bf16[3,256,128]{2,1,0:T(8,128)(2,1)S(1)}, bf16[3,256,128]{2,1,0:T(8,128)(2,1)S(1)}, u32[]{:S(2)}, u32[]{:S(2)}) collective-permute-start(bf16[3,256,128]{2,1,0:T(8,128)(2,1)S(1)} %broadcast_select_fusion.1), channel_id=1, source_target_pairs={{32,0},{48,16},{64,32},{80,48},{96,64},{112,80},{128,96},{144,112}... | collective-permute-start | bytes 589832 | tf_op jit(solution)/shard_map/ppermute | solution.py:12
  49.6 15.5 %collective-permute-start.4 = (bf16[3,256,128]{2,1,0:T(8,128)(2,1)S(1)}, bf16[3,256,128]{2,1,0:T(8,128)(2,1)S(1)}, u32[]{:S(2)}, u32[]{:S(2)}) collective-permute-start(bf16[3,256,128]{2,1,0:T(8,128)(2,1)S(1)} %broadcast_select_fusion.6), channel_id=1, source_target_pairs={{0,32},{16,48},{32,64},{48,80},{64,96},{80,112},{96,128},{112,144}... | collective-permute-start | bytes 589832 | tf_op jit(solution)/shard_map/ppermute | solution.py:12
  54.7 10.5 %collective-permute-start.5 = (bf16[3,256,128]{2,1,0:T(8,128)(2,1)S(1)}, bf16[3,256,128]{2,1,0:T(8,128)(2,1)S(1)}, u32[]{:S(2)}, u32[]{:S(2)}) collective-permute-start(bf16[3,256,128]{2,1,0:T(8,128)(2,1)S(1)} %broadcast_select_fusion.4), channel_id=1, source_target_pairs={{0,16},{16,32},{32,48},{48,64},{64,80},{80,96},{96,112},{112,128},... | collective-permute-start | bytes 589832 | tf_op jit(solution)/shard_map/ppermute | solution.py:12
  61.1 8.5 %collective-permute-start.6 = (bf16[3,256,128]{2,1,0:T(8,128)(2,1)S(1)}, bf16[3,256,128]{2,1,0:T(8,128)(2,1)S(1)}, u32[]{:S(2)}, u32[]{:S(2)}) collective-permute-start(bf16[3,256,128]{2,1,0:T(8,128)(2,1)S(1)} %broadcast_select_fusion.2), channel_id=1, source_target_pairs={{16,0},{32,16},{48,32},{64,48},{80,64},{96,80},{112,96},{128,112},... | collective-permute-start | bytes 589832 | tf_op jit(solution)/shard_map/ppermute | solution.py:12
  63.2 9.4 %collective-permute-start.7 = (bf16[3,256,128]{2,1,0:T(8,128)(2,1)S(1)}, bf16[3,256,128]{2,1,0:T(8,128)(2,1)S(1)}, u32[]{:S(2)}, u32[]{:S(2)}) collective-permute-start(bf16[3,256,128]{2,1,0:T(8,128)(2,1)S(1)} %broadcast_select_fusion), channel_id=1, source_target_pairs={{32,0},{48,16},{64,32},{80,48},{96,64},{112,80},{128,96},{144,112}... | collective-permute-start | bytes 589832 | tf_op jit(solution)/shard_map/ppermute | solution.py:12
  87.7 21.8 %copy-start.2 = (bf16[32,512]{1,0:T(8,128)(2,1)S(1)}, bf16[32,512]{1,0:T(8,128)(2,1)}, u32[]{:S(2)}) copy-start(bf16[32,512]{1,0:T(8,128)(2,1)} %param.14) | copy-start | bytes 98308
  98.0 50.0 %all-to-all-start = ((bf16[16,8,32,128]{3,2,1,0:T(8,128)(2,1)}), bf16[16,8,32,128]{3,2,1,0:T(8,128)(2,1)S(1)}, u32[]{:S(2)}, u32[]{:S(2)}) async-start(bf16[16,8,32,128]{3,2,1,0:T(8,128)(2,1)} %fusion.22), calls=%async_computation | async-start | bytes 2097152 | tf_op jit(solution)/shard_map/all_to_all | solution.py:49
